TPU v7x, 512 devices: a whole 4x8x8 slice. The times are simulated.
512 devices in a mesh: segment: 2 (over core), mp: 64 (over y, z), dp: 4 (over x).
Axes of the slice: x: 4, y: 8, z: 8, core: 2. Of those that a mesh axis runs over, the one named last changes fastest.
Arguments:
- key_value: bfloat16 [8, 128, 96, 2048], P('dp', ('segment', 'mp')), may hold values from -5 to 5
- key_gain: float32 [128], replicated, may hold values from 0.1 to 1.9
- queries: bfloat16 [8, 32, 32, 8192], P('dp', 'segment', None, 'mp'), may hold values from -36 to 36
- tile_count: int32 [8, 32, 32], P('dp', 'segment'), may hold values from 0 to 4
- attn_gate: float32 [1], replicated, may hold values from 0.3 to 1.2
- cotangent: bfloat16 [8, 32, 32, 8192], P('dp', 'segment', None, 'mp'), may hold values from -6 to 6
Outputs:
- attended: bfloat16 [8, 32, 32, 8192], P('dp', 'segment', None, 'mp')
- d_key_value: bfloat16 [8, 128, 96, 2048], P('dp', ('segment', 'mp'))
- d_gain: float32 [128], replicated
- d_gate: float32 [1], replicated
Inputs may be any that keep to these rules, and one draw needn't show every extreme that they name: A text token sees the first tile_count tiles of its own sample's image; 0 means it sees none and its output is zero.
All inputs are finite; a program needn't handle non-finite values.
Results may differ from a plain program's by a relative error of at most 0.0034.
The roundings to bfloat16 on the way count: a program that leaves them out, or rounds other values in their place, can miss the bound.
Values may be sent and summed in bfloat16 or wider, within the bound.
A program may use at most 64 MiB of HBM per device.

v0:
```python
import jax
import jax.numpy as jnp
from jax import lax
from jax.sharding import PartitionSpec as P

HEADS = 64
KV_HEADS = 8
HEAD = 128
TILES = 4
PATCH = 96
MICRO = 2


def shards(key_value, key_gain, queries, tile_count, attn_gate, cotangent):
    n_model = lax.axis_size("mp")
    per_device = HEADS // n_model
    group = HEADS // KV_HEADS
    kv_local = max(1, per_device // group)
    local_group = per_device // kv_local
    blocks = KV_HEADS // kv_local
    copies = n_model // blocks
    tiles_dev = key_value.shape[1]
    rows_dev = tiles_dev * key_value.shape[2]
    samples = queries.shape[1]
    text = queries.shape[2]
    keys_all = TILES * PATCH
    pieces = keys_all // rows_dev
    wide = kv_local * 2 * HEAD
    scale = 1.0 / HEAD**0.5
    gate = jnp.tanh(attn_gate[0])
    key_tile = lax.broadcasted_iota(jnp.int32, (1, 1, keys_all), 2) // PATCH
    outputs = []
    grad_rows = []
    d_gain = jnp.zeros((HEAD,), jnp.float32)
    gate_total = jnp.zeros((), jnp.float32)
    for micro in range(MICRO):
        states = key_value[micro].reshape(rows_dev, KV_HEADS, 2, HEAD)
        raw_key = states[:, :, 0].astype(jnp.float32)
        encode_inverse = lax.rsqrt(jnp.mean(raw_key * raw_key, axis=-1, keepdims=True) + 1e-05)
        encode_unit_key = raw_key * encode_inverse
        normed = jnp.stack(
            [(encode_unit_key * key_gain).astype(jnp.bfloat16), states[:, :, 1]], axis=2
        )
        outgoing = jnp.repeat(normed.reshape(rows_dev, blocks, wide), copies, axis=1)
        outgoing, unit_key, inverse = (outgoing, encode_unit_key, encode_inverse)
        arrived = lax.all_to_all(outgoing, "mp", split_axis=1, concat_axis=0, tiled=True)
        kv_heads = arrived.reshape(samples, keys_all, kv_local, 2, HEAD)
        keys = kv_heads[:, :, :, 0]
        values = kv_heads[:, :, :, 1]
        query_heads = queries[micro].reshape(samples, text, kv_local, local_group, HEAD)
        logits = (
            jnp.einsum("stkgd,snkd->skgtn", query_heads, keys, preferred_element_type=jnp.float32)
            * scale
        )
        counts = tile_count[micro]
        allowed = key_tile < jnp.maximum(counts, 1)[:, :, None]
        logits = jnp.where(allowed[:, None, None], logits, -1e30)
        top = jnp.max(logits, axis=-1, keepdims=True)
        exps = jnp.exp(logits - top)
        probs = exps / jnp.sum(exps, axis=-1, keepdims=True)
        probs_low = probs.astype(jnp.bfloat16)
        mixed = jnp.einsum(
            "skgtn,snkd->stkgd", probs_low, values, preferred_element_type=jnp.float32
        )
        live = (counts > 0).astype(jnp.float32)[:, :, None, None, None]
        attended = (
            (gate * live * mixed).astype(jnp.bfloat16).reshape(samples, text, per_device * HEAD)
        )
        cotan_heads = (
            cotangent[micro].reshape(samples, text, kv_local, local_group, HEAD).astype(jnp.float32)
        )
        gate_part = jnp.sum(cotan_heads * live * mixed)
        d_mixed = (gate * live * cotan_heads).astype(jnp.bfloat16)
        d_probs = jnp.einsum(
            "stkgd,snkd->skgtn", d_mixed, values, preferred_element_type=jnp.float32
        )
        inner = jnp.sum(probs * d_probs, axis=-1, keepdims=True)
        d_logits = (probs * (d_probs - inner) * scale).astype(jnp.bfloat16)
        split_shape = (samples, kv_local, local_group, text, pieces, rows_dev)
        d_keys = jnp.einsum(
            "skgtar,stkgd->sakgrd",
            d_logits.reshape(split_shape),
            query_heads,
            preferred_element_type=jnp.float32,
        ).astype(jnp.bfloat16)
        d_values = jnp.einsum(
            "skgtar,stkgd->sakgrd",
            probs_low.reshape(split_shape),
            d_mixed,
            preferred_element_type=jnp.float32,
        ).astype(jnp.bfloat16)
        back = jnp.concatenate([d_keys, d_values], axis=-1).reshape(
            n_model, per_device, rows_dev, 2 * HEAD
        )
        attended, back, gate_part = (attended, back, gate_part)
        returned = lax.all_to_all(back, "mp", split_axis=0, concat_axis=1, tiled=True)[0]
        summed = jnp.sum(
            returned.astype(jnp.float32).reshape(KV_HEADS, group, rows_dev, 2 * HEAD), axis=1
        )
        summed = jnp.swapaxes(summed.astype(jnp.bfloat16), 0, 1)
        key_part = summed[:, :, :HEAD].astype(jnp.float32)
        gain_part = jnp.sum(key_part * unit_key, axis=(0, 1))
        scaled = key_part * key_gain
        d_unit = inverse * (scaled - unit_key * jnp.mean(scaled * unit_key, axis=-1, keepdims=True))
        d_rows = jnp.concatenate([d_unit.astype(jnp.bfloat16), summed[:, :, HEAD:]], axis=-1)
        d_rows, gain_part = (d_rows.reshape(tiles_dev, PATCH, KV_HEADS * 2 * HEAD), gain_part)
        outputs.append(attended)
        grad_rows.append(d_rows)
        d_gain = d_gain + gain_part
        gate_total = gate_total + gate_part
    d_gain, gate_total = lax.psum((d_gain, gate_total), ("segment", "mp", "dp"))
    d_gate = (gate_total * (1.0 - gate * gate)).reshape(1)
    return (jnp.stack(outputs, axis=0), jnp.stack(grad_rows, axis=0), d_gain, d_gate)


def solution(mesh):
    in_specs = (
        P("dp", ("segment", "mp"), None, None),
        P(),
        P("dp", "segment", None, "mp"),
        P("dp", "segment", None),
        P(),
        P("dp", "segment", None, "mp"),
    )
    out_specs = (P("dp", "segment", None, "mp"), P("dp", ("segment", "mp"), None, None), P(), P())
    return jax.shard_map(shards, mesh=mesh, in_specs=in_specs, out_specs=out_specs, check_vma=False)
```

profile of v0, /device:TPU:1, one launch (start us, length us, event | category | flops | bytes accessed | tf_op | source)
XLA Modules:
  0.0 521.8 jit_solution(4912235641572588195)
XLA Ops:
  0.6 1.2 fusion.79
  5.3 2.0 broadcast_in_dim.9
  7.4 17.1 %all-to-all-start = ((bf16[96,64,256]{2,0,1:T(8,128)(2,1)}), bf16[96,64,256]{2,0,1:T(8,128)(2,1)S(1)}, u32[]{:S(2)}, u32[]{:S(2)}) async-start(bf16[96,64,256]{2,0,1:T(8,128)(2,1)} %bitcast.280), calls=%async_computation | async-start | bytes 6291456 | tf_op jit(solution)/shard_map/all_to_all | solution.py:46
  24.8 85.7 %all-to-all-done = bf16[96,64,256]{2,0,1:T(8,128)(2,1)S(1)} async-done(((bf16[96,64,256]{2,0,1:T(8,128)(2,1)}), bf16[96,64,256]{2,0,1:T(8,128)(2,1)S(1)}, u32[]{:S(2)}, u32[]{:S(2)}) %all-to-all-start) | async-done | bytes 3145760 | tf_op jit(solution)/shard_map/all_to_all | solution.py:46
  110.5 2.3 broadcast_in_dim.11
  113.1 20.4 %all-to-all-start.1 = ((bf16[96,64,256]{2,0,1:T(8,128)(2,1)}), bf16[96,64,256]{2,0,1:T(8,128)(2,1)}, u32[]{:S(2)}, u32[]{:S(2)}) async-start(bf16[96,64,256]{2,0,1:T(8,128)(2,1)} %bitcast.20), calls=%async_computation.1 | async-start | bytes 6291456 | tf_op jit(solution)/shard_map/all_to_all | solution.py:46
  134.8 3.8 reshape.332
  138.6 5.7 %fusion.77 = (bf16[16,384,1,1,128]{4,3,1,0,2:T(2,128)(2,1)S(1)}, bf16[16,384,1,1,128]{4,3,1,0,2:T(2,128)(2,1)S(1)}) fusion(bf16[16,384,1,2,128]{4,3,1,0,2:T(2,128)(2,1)S(1)} %reshape.332), kind=kLoop, calls=%fused_computation.133 | loop fusion | bytes 6291456 | tf_op jit(solution)/shard_map/slice | solution.py:48
  144.4 0.7 fusion.83
  145.5 0.8 multiply_reduce_fusion.1
  147.8 0.8 fusion.3
  148.5 0.6 fusion.2
  149.2 2.1 pad_maximum_fusion
  151.3 60.0 %all-to-all-done.1 = bf16[96,64,256]{2,0,1:T(8,128)(2,1)} async-done(((bf16[96,64,256]{2,0,1:T(8,128)(2,1)}), bf16[96,64,256]{2,0,1:T(8,128)(2,1)}, u32[]{:S(2)}, u32[]{:S(2)}) %all-to-all-start.1) | async-done | bytes 3145760 | tf_op jit(solution)/shard_map/all_to_all | solution.py:46
  211.3 21.5 %all-to-all-start.2 = ((bf16[64,1,96,256]{3,2,1,0:T(8,128)(2,1)}), bf16[64,1,96,256]{3,2,1,0:T(8,128)(2,1)}, u32[]{:S(2)}, u32[]{:S(2)}) async-start(bf16[64,1,96,256]{3,2,1,0:T(8,128)(2,1)} %bitcast.47), calls=%async_computation.2 | async-start | bytes 6291456 | tf_op jit(solution)/shard_map/all_to_all | solution.py:96
  232.8 3.8 reshape.339
  236.6 5.7 %fusion.78 = (bf16[16,384,1,1,128]{4,3,1,0,2:T(2,128)(2,1)S(1)}, bf16[16,384,1,1,128]{4,3,1,0,2:T(2,128)(2,1)S(1)}) fusion(bf16[16,384,1,2,128]{4,3,1,0,2:T(2,128)(2,1)S(1)} %reshape.339), kind=kLoop, calls=%fused_computation.134 | loop fusion | bytes 6291456 | tf_op jit(solution)/shard_map/slice | solution.py:48
  242.4 0.7 fusion.82
  243.5 0.8 multiply_reduce_fusion
  245.4 0.8 fusion.5
  246.8 2.2 pad_maximum_fusion.1
  249.0 60.8 %all-to-all-done.2 = bf16[64,1,96,256]{3,2,1,0:T(8,128)(2,1)} async-done(((bf16[64,1,96,256]{3,2,1,0:T(8,128)(2,1)}), bf16[64,1,96,256]{3,2,1,0:T(8,128)(2,1)}, u32[]{:S(2)}, u32[]{:S(2)}) %all-to-all-start.2) | async-done | bytes 3145760 | tf_op jit(solution)/shard_map/all_to_all | solution.py:96
  309.8 16.2 %all-to-all-start.3 = ((bf16[64,1,96,256]{3,2,1,0:T(8,128)(2,1)}), bf16[64,1,96,256]{3,2,1,0:T(8,128)(2,1)S(1)}, u32[]{:S(2)}, u32[]{:S(2)}) async-start(bf16[64,1,96,256]{3,2,1,0:T(8,128)(2,1)} %bitcast.64), calls=%async_computation.3 | async-start | bytes 6291456 | tf_op jit(solution)/shard_map/all_to_all | solution.py:96
  326.0 2.3 convolution_bitcast_fusion.2
  328.3 3.7 fusion.55
  333.3 1.6 pad_maximum_fusion.7
  334.9 2.4 bitcast_reduce_fusion.1
  337.3 0.7 slice.89
  338.1 0.7 fusion.42
  338.8 68.5 %all-to-all-done.3 = bf16[64,1,96,256]{3,2,1,0:T(8,128)(2,1)S(1)} async-done(((bf16[64,1,96,256]{3,2,1,0:T(8,128)(2,1)}), bf16[64,1,96,256]{3,2,1,0:T(8,128)(2,1)S(1)}, u32[]{:S(2)}, u32[]{:S(2)}) %all-to-all-start.3) | async-done | bytes 3145760 | tf_op jit(solution)/shard_map/all_to_all | solution.py:96
  410.1 0.9 pad_maximum_fusion.2
  411.1 108.9 %all-reduce = (f32[128]{0:T(128)}, f32[]{:T(128)}) all-reduce(f32[128]{0:T(128)S(1)} %add.34, f32[]{:T(128)S(6)} %add.35), channel_id=1, replica_groups=mesh['segment'=2,'mp'=64,'dp'=4] {'segment','mp','dp'}, use_global_device_ids=true, to_apply=%region_14.15 | all-reduce | flops 129 | bytes 1032 | tf_op jit(solution)/shard_map/psum | solution.py:111
  (82 shorter events, 11.2 us)
Async XLA Ops:
  2.1 2.6 copy-start.17
  3.0 2.3 copy-start.3
  4.0 0.7 copy-start.5
  7.4 103.1 %all-to-all-start = ((bf16[96,64,256]{2,0,1:T(8,128)(2,1)}), bf16[96,64,256]{2,0,1:T(8,128)(2,1)S(1)}, u32[]{:S(2)}, u32[]{:S(2)}) async-start(bf16[96,64,256]{2,0,1:T(8,128)(2,1)} %bitcast.280), calls=%async_computation | async-start | bytes 6291456 | tf_op jit(solution)/shard_map/all_to_all | solution.py:46
  110.5 2.6 copy-start
  112.8 21.4 %copy-start.15 = (s32[2,16,32]{2,1,0:T(8,128)S(1)}, s32[2,16,32]{2,1,0:T(8,128)}, u32[]{:S(2)}) copy-start(s32[2,16,32]{2,1,0:T(8,128)} %param.9) | copy-start | bytes 12292
  113.1 98.2 %all-to-all-start.1 = ((bf16[96,64,256]{2,0,1:T(8,128)(2,1)}), bf16[96,64,256]{2,0,1:T(8,128)(2,1)}, u32[]{:S(2)}, u32[]{:S(2)}) async-start(bf16[96,64,256]{2,0,1:T(8,128)(2,1)} %bitcast.20), calls=%async_computation.1 | async-start | bytes 6291456 | tf_op jit(solution)/shard_map/all_to_all | solution.py:46
  134.8 12.9 %copy-start.16 = (f32[16,32]{1,0:T(8,128)}, f32[16,32]{1,0:T(8,128)S(1)}, u32[]{:S(2)}) copy-start(f32[16,32]{1,0:T(8,128)S(1)} %get-tuple-element.54) | copy-start | bytes 6148
  138.6 5.8 %copy-start.11 = (bf16[2,16,32,128]{3,2,1,0:T(8,128)(2,1)S(1)}, bf16[2,16,32,128]{3,2,1,0:T(8,128)(2,1)}, u32[]{:S(2)}) copy-start(bf16[2,16,32,128]{3,2,1,0:T(8,128)(2,1)} %param.8) | copy-start | bytes 786436
  144.4 1.9 copy-start.2
  144.4 1.1 copy-start.13
  146.6 0.7 copy-start.9
  211.3 98.5 %all-to-all-start.2 = ((bf16[64,1,96,256]{3,2,1,0:T(8,128)(2,1)}), bf16[64,1,96,256]{3,2,1,0:T(8,128)(2,1)}, u32[]{:S(2)}, u32[]{:S(2)}) async-start(bf16[64,1,96,256]{3,2,1,0:T(8,128)(2,1)} %bitcast.47), calls=%async_computation.2 | async-start | bytes 6291456 | tf_op jit(solution)/shard_map/all_to_all | solution.py:96
  242.4 1.9 copy-start.1
  242.4 1.1 copy-start.14
  244.3 1.8 copy-start.12
  309.8 97.5 %all-to-all-start.3 = ((bf16[64,1,96,256]{3,2,1,0:T(8,128)(2,1)}), bf16[64,1,96,256]{3,2,1,0:T(8,128)(2,1)S(1)}, u32[]{:S(2)}, u32[]{:S(2)}) async-start(bf16[64,1,96,256]{3,2,1,0:T(8,128)(2,1)} %bitcast.64), calls=%async_computation.3 | async-start | bytes 6291456 | tf_op jit(solution)/shard_map/all_to_all | solution.py:96
  328.2 9.9 %copy-start.4 = (bf16[96,8,1,128]{3,0,1,2:T(8,128)(2,1)S(1)}, bf16[96,8,1,128]{3,0,1,2:T(8,128)(2,1)}, u32[]{:S(2)}) copy-start(bf16[96,8,1,128]{3,0,1,2:T(8,128)(2,1)} %copy-done.3) | copy-start | bytes 589828
  332.0 6.2 %copy-start.18 = (f32[128]{0:T(128)S(1)}, f32[128]{0:T(128)}, u32[]{:S(2)}) copy-start(f32[128]{0:T(128)} %param.7) | copy-start | bytes 1540
  337.3 0.8 copy-start.7
  337.3 70.6 %copy-start.6 = (bf16[96,8,1,128]{3,0,1,2:T(8,128)(2,1)S(1)}, bf16[96,8,1,128]{3,0,1,2:T(8,128)(2,1)}, u32[]{:S(2)}) copy-start(bf16[96,8,1,128]{3,0,1,2:T(8,128)(2,1)} %copy-done.5) | copy-start | bytes 589828
  407.3 1.0 copy-start.8
  407.8 1.8 copy-start.10
  409.1 1.9 copy-start.19
where the time goes:
time: 523 us; the launch traced here: 522 us
  waiting for transfers between devices  275 us (53%)
  blocking collectives  109 us (21%)
  starting transfers between devices  75.2 us (14%)
  local copies, waits for them, and re-layouts  31.7 us (6%)
  other arithmetic  14.2 us (3%)
  matrix products  11.9 us (2%)
    all_to_all x2, waiting for transfers between devices, shards(): lax.all_to_all(outgoing, 'mp', split_axis=1, concat_axis=0, tiled=True)  146 us
    all_to_all x2, waiting for transfers between devices, shards(): lax.all_to_all(back, 'mp', split_axis=0, concat_axis=1, tiled=True)[0]  129 us
    psum x1, blocking collectives, shards(): d_gain, gate_total = lax.psum((d_gain, gate_total), ('segment', 'mp', 'dp'))  109 us
    all_to_all x2, starting transfers between devices, shards(): lax.all_to_all(back, 'mp', split_axis=0, concat_axis=1, tiled=True)[0]  37.7 us
    all_to_all x2, starting transfers between devices, shards(): lax.all_to_all(outgoing, 'mp', split_axis=1, concat_axis=0, tiled=True)  37.5 us
    slice x2, local copies, waits for them, and re-layouts, shards(): keys = kv_heads[:, :, :, 0]  11.5 us
  transfers between devices with their start and end apart: 4, of which 4 were waited for; matrix products, arithmetic and copies ran while one was open for 8% of the time, Pallas kernels for 0%

commit v1 on v0

v1 whole, which is shorter than its diff:
```python
import jax
import jax.numpy as jnp
from jax import lax
from jax.experimental import pallas as pl
from jax.experimental.pallas import tpu as pltpu
from jax.sharding import PartitionSpec as P

HEAD = 128
TILES = 4
PATCH = 96
KEYS = TILES * PATCH
MICRO = 2
SAMPLES = 16
TEXT = 32
GROUP = 8
OWN_KV = 2
OWN_HEADS = OWN_KV * GROUP
ROWS = GROUP * TEXT
WIDE = 2 * HEAD
SCALE = 1.0 / HEAD**0.5


def dot(a, b, dims):
    return lax.dot_general(a, b, (dims, ((), ())), preferred_element_type=jnp.float32)


def kernel(
    kv_ref, gain_ref, q_ref, count_ref, gate_ref, cot_ref,
    att_ref, dkv_ref, dgain_ref, dgate_ref,
    kvbuf, qbuf, cbuf, gbuf, abuf, qblk, dblk, red_src, red1, red2, red3,
    kv_send, kv_recv, q_send, q_recv, c_send, c_recv, g_send, g_recv, a_send, a_recv,
    r1_send, r1_recv, r2_send, r2_recv, r3_send, r3_recv,
):
    me = lax.axis_index("mp")
    seg = lax.axis_index("segment")
    dp = lax.axis_index("dp")
    n_dp = lax.axis_size("dp")
    n_rep = n_dp * lax.axis_size("segment")
    sample = me // TILES
    place = me % TILES
    part = (place + TILES - (sample // 2) % TILES) % TILES
    my_part = me // OWN_HEADS
    my_slot = me % OWN_HEADS
    my_unit = my_slot // GROUP
    rep = dp * lax.axis_size("segment") + seg

    def worker(n):
        return n * TILES + (my_part + n // 2) % TILES

    def owner(i):
        return part * OWN_HEADS + i

    def member(i):
        return sample * TILES + i

    def member_part(i):
        return (i + TILES - (sample // 2) % TILES) % TILES

    def rep_id(i):
        return {"segment": i % lax.axis_size("segment"), "dp": i // lax.axis_size("segment")}

    barrier = pltpu.get_barrier_semaphore()
    has_self = (part == my_part).astype(jnp.int32)

    def greet_heads(i, _):
        @pl.when(worker(i) != me)
        def _():
            pl.semaphore_signal(barrier, inc=1, device_id={"mp": worker(i)})

        @pl.when(owner(i) != me)
        def _():
            pl.semaphore_signal(barrier, inc=1, device_id={"mp": owner(i)})
        return 0

    def greet_members(i, _):
        @pl.when(i != place)
        def _():
            pl.semaphore_signal(barrier, inc=1, device_id={"mp": member(i)})
        return 0

    def greet_reps(i, _):
        @pl.when(i != rep)
        def _():
            pl.semaphore_signal(barrier, inc=1, device_id=rep_id(i))
        return 0

    lax.fori_loop(0, TILES, greet_members, 0)
    lax.fori_loop(0, SAMPLES, greet_heads, 0)
    lax.fori_loop(0, n_rep, greet_reps, 0)
    qblk[...] = jnp.zeros_like(qblk)
    dblk[...] = jnp.zeros_like(dblk)
    pl.semaphore_wait(barrier, 2 * (SAMPLES - has_self) + TILES - 1 + n_rep - 1)

    def columns(p, u):
        return pl.ds(pl.multiple_of((p * OWN_KV + u) * WIDE, WIDE), WIDE)

    def kv_copy(b, u, i):
        return pltpu.make_async_remote_copy(
            kv_ref.at[b, 0, :, columns(member_part(i), u)], kvbuf.at[b, u, place],
            kv_send.at[b, u, i], kv_recv.at[b, u], device_id={"mp": member(i)},
        )

    def q_copy(b, n):
        return pltpu.make_async_remote_copy(
            q_ref.at[b, n], qbuf.at[b, my_slot], q_send.at[b, n], q_recv.at[b, my_unit],
            device_id={"mp": worker(n)},
        )

    def c_copy(b, n):
        return pltpu.make_async_remote_copy(
            cot_ref.at[b, n], cbuf.at[b, my_slot], c_send.at[b, n], c_recv.at[b, my_unit],
            device_id={"mp": worker(n)},
        )

    def send_kv(b, u):
        def step(i, _):
            @pl.when(i != place)
            def _():
                kv_copy(b, u, i).start()
            return 0
        lax.fori_loop(0, TILES, step, 0)
        pltpu.make_async_copy(
            kv_ref.at[b, 0, :, columns(part, u)], kvbuf.at[b, u, place], kv_recv.at[b, u]
        ).start()

    def send_heads(b):
        def q_step(n, _):
            @pl.when(worker(n) != me)
            def _():
                q_copy(b, n).start()

            @pl.when(worker(n) == me)
            def _():
                pltpu.make_async_copy(q_ref.at[b, n], qbuf.at[b, my_slot], q_recv.at[b, my_unit]).start()
            return 0

        def c_step(n, _):
            @pl.when(worker(n) != me)
            def _():
                c_copy(b, n).start()

            @pl.when(worker(n) == me)
            def _():
                pltpu.make_async_copy(cot_ref.at[b, n], cbuf.at[b, my_slot], c_recv.at[b, my_unit]).start()
            return 0

        lax.fori_loop(0, SAMPLES, q_step, 0)
        lax.fori_loop(0, SAMPLES, c_step, 0)

    for b in range(MICRO):
        send_kv(b, 0)
        send_heads(b)
        send_kv(b, 1)

    gate = jnp.tanh(jnp.full((1, HEAD), gate_ref[0], jnp.float32))
    gain = gain_ref[...]
    token_of = (lax.broadcasted_iota(jnp.int32, (ROWS, TEXT), 0) & (TEXT - 1)) == (
        lax.broadcasted_iota(jnp.int32, (ROWS, TEXT), 1)
    )
    spread = token_of.astype(jnp.bfloat16)
    key_row = lax.broadcasted_iota(jnp.int32, (KEYS, ROWS), 0)

    def g_copy(b, u, i):
        return pltpu.make_async_remote_copy(
            gbuf.at[b, u, i], dkv_ref.at[b, 0, :, columns(part, u)], g_send.at[b, u, i], g_recv.at[0],
            device_id={"mp": member(i)},
        )

    def a_copy(b, i):
        return pltpu.make_async_remote_copy(
            abuf.at[b, i], att_ref.at[b, sample], a_send.at[b, i], a_recv.at[0],
            device_id={"mp": owner(i)},
        )

    def unit(step, carry):
        gain_sum, gate_sum = carry
        b = step // OWN_KV
        u = step % OWN_KV
        heads = pl.ds(u * GROUP, GROUP)
        q_view, c_view = qbuf.at[b, heads], cbuf.at[b, heads]
        counts = count_ref[b, pl.ds(sample, 1), :].astype(jnp.float32).astype(jnp.bfloat16)
        count_col = dot(spread, jnp.broadcast_to(counts, (HEAD, TEXT)), ((1,), (1,)))
        count_row = dot(jnp.broadcast_to(counts, (8, TEXT)), spread, ((1,), (1,)))[0:1]
        live = (count_col > 0.5).astype(jnp.float32)
        gate_live = gate * live
        limit = (jnp.maximum(count_row, 1.0) * PATCH).astype(jnp.int32)

        pltpu.make_async_copy(kvbuf.at[b, u], kvbuf.at[b, u], kv_recv.at[b, u]).wait()
        kv = kvbuf[b, u].reshape(KEYS, WIDE)
        raw = kv[:, :HEAD].astype(jnp.float32)
        values = kv[:, HEAD:]
        inverse = lax.rsqrt(jnp.mean(raw * raw, axis=-1, keepdims=True) + 1e-05)
        unit_key = raw * inverse
        keys = (unit_key * gain).astype(jnp.bfloat16)

        pltpu.make_async_copy(q_view, q_view, q_recv.at[b, u]).wait()
        queries = q_view[...].reshape(ROWS, HEAD)
        logits = dot(keys, queries, ((1,), (1,))) * SCALE
        logits = jnp.where(key_row < limit, logits, -1e30)
        exps = jnp.exp(logits - jnp.max(logits, axis=0, keepdims=True))
        probs = exps / jnp.sum(exps, axis=0, keepdims=True)
        probs_low = probs.astype(jnp.bfloat16)
        mixed = dot(probs_low, values, ((0,), (0,)))
        abuf[b, heads] = (gate_live * mixed).astype(jnp.bfloat16).reshape(GROUP, TEXT, HEAD)

        def a_step(k, _):
            i = u * GROUP + k

            @pl.when(owner(i) != me)
            def _():
                a_copy(b, i).start()

            @pl.when(owner(i) == me)
            def _():
                pltpu.make_async_copy(abuf.at[b, i], att_ref.at[b, sample], a_recv.at[0]).start()
            return 0

        lax.fori_loop(0, GROUP, a_step, 0)

        pltpu.make_async_copy(c_view, c_view, c_recv.at[b, u]).wait()
        cotan = c_view[...].reshape(ROWS, HEAD).astype(jnp.float32)
        gate_sum = gate_sum + jnp.sum(cotan * live * mixed, axis=0, keepdims=True)
        d_mixed = (gate_live * cotan).astype(jnp.bfloat16)
        d_probs = dot(values, d_mixed, ((1,), (1,)))
        inner = jnp.sum(probs * d_probs, axis=0, keepdims=True)
        d_logits = (probs * (d_probs - inner) * SCALE).astype(jnp.bfloat16)
        for h in range(GROUP):
            rows, cols = slice(h * TEXT, (h + 1) * TEXT), slice(h * HEAD, (h + 1) * HEAD)
            qblk[rows, cols] = queries[rows]
            dblk[rows, cols] = d_mixed[rows]

        def head_sum(left, blocks):
            total = jnp.zeros((KEYS, HEAD), jnp.float32)
            for h in range(0, GROUP, 2):
                pair = dot(left, blocks[:, h * HEAD:(h + 2) * HEAD], ((1,), (0,)))
                pair = pair.astype(jnp.bfloat16).astype(jnp.float32)
                total = total + pair[:, :HEAD] + pair[:, HEAD:]
            return total.astype(jnp.bfloat16)

        key_part = head_sum(d_logits, qblk).astype(jnp.float32)
        value_part = head_sum(probs_low, dblk)
        gain_sum = gain_sum + jnp.sum(key_part * unit_key, axis=0, keepdims=True)
        scaled = key_part * gain
        d_key = inverse * (scaled - unit_key * jnp.mean(scaled * unit_key, axis=-1, keepdims=True))
        gbuf[b, u, :, :, :HEAD] = d_key.astype(jnp.bfloat16).reshape(TILES, PATCH, HEAD)
        gbuf[b, u, :, :, HEAD:] = value_part.reshape(TILES, PATCH, HEAD)

        def g_step(i, _):
            @pl.when(i != place)
            def _():
                g_copy(b, u, i).start()
            return 0

        lax.fori_loop(0, TILES, g_step, 0)
        pltpu.make_async_copy(
            gbuf.at[b, u, place], dkv_ref.at[b, 0, :, columns(part, u)], g_recv.at[0]
        ).start()
        return gain_sum, gate_sum

    zero = jnp.zeros((1, HEAD), jnp.float32)
    gain_sum, gate_sum = lax.fori_loop(0, MICRO * OWN_KV, unit, (zero, zero))

    row = lax.broadcasted_iota(jnp.int32, (8, HEAD), 0)

    def spread_sums(gain_sum, gate_sum):
        return jnp.where(row == 0, gain_sum, jnp.where(row == 1, gate_sum, 0.0))

    red_src[0] = spread_sums(gain_sum, gate_sum)

    def r1_copy(n):
        return pltpu.make_async_remote_copy(
            red_src.at[0], red1.at[my_slot], r1_send.at[n], r1_recv.at[0], device_id={"mp": worker(n)}
        )

    def r1_step(n, _):
        @pl.when(worker(n) != me)
        def _():
            r1_copy(n).start()

        @pl.when(worker(n) == me)
        def _():
            pltpu.make_async_copy(red_src.at[0], red1.at[my_slot], r1_recv.at[0]).start()
        return 0

    lax.fori_loop(0, SAMPLES, r1_step, 0)
    pltpu.make_async_copy(red1, red1, r1_recv.at[0]).wait()
    red_src[1] = jnp.sum(red1[...], axis=0)

    def r2_copy(i):
        return pltpu.make_async_remote_copy(
            red_src.at[1], red2.at[place], r2_send.at[i], r2_recv.at[0], device_id={"mp": member(i)}
        )

    def r2_step(i, _):
        @pl.when(i != place)
        def _():
            r2_copy(i).start()
        return 0

    lax.fori_loop(0, TILES, r2_step, 0)
    pltpu.make_async_copy(red_src.at[1], red2.at[place], r2_recv.at[0]).start()
    pltpu.make_async_copy(red2, red2, r2_recv.at[0]).wait()
    red_src[2] = jnp.sum(red2[...], axis=0)

    def r3_copy(i):
        return pltpu.make_async_remote_copy(
            red_src.at[2], red3.at[rep], r3_send.at[i], r3_recv.at[0], device_id=rep_id(i)
        )

    def r3_step(i, _):
        @pl.when(i != rep)
        def _():
            r3_copy(i).start()
        return 0

    lax.fori_loop(0, n_rep, r3_step, 0)
    pltpu.make_async_copy(red_src.at[2], red3.at[rep], r3_recv.at[0]).start()

    def heads_sent(n, _):
        @pl.when(worker(n) != me)
        def _():
            for b in range(MICRO):
                q_copy(b, n).wait_send()
                c_copy(b, n).wait_send()
            r1_copy(n).wait_send()

        @pl.when(owner(n) != me)
        def _():
            for b in range(MICRO):
                a_copy(b, n).wait_send()
        return 0

    def members_sent(i, _):
        @pl.when(i != place)
        def _():
            for b in range(MICRO):
                for u in range(OWN_KV):
                    kv_copy(b, u, i).wait_send()
                    g_copy(b, u, i).wait_send()
            r2_copy(i).wait_send()
        return 0

    def reps_sent(i, _):
        @pl.when(i != rep)
        def _():
            r3_copy(i).wait_send()
        return 0

    lax.fori_loop(0, SAMPLES, heads_sent, 0)
    lax.fori_loop(0, TILES, members_sent, 0)
    lax.fori_loop(0, n_rep, reps_sent, 0)

    pltpu.make_async_copy(red3, red3, r3_recv.at[0]).wait()
    total = jnp.sum(red3[...], axis=0)
    dgain_ref[...] = total[0:1]
    dgate_ref[...] = jnp.sum(total[1:2], axis=1, keepdims=True) * (1.0 - gate * gate)

    pltpu.make_async_copy(att_ref, att_ref, a_recv.at[0]).wait()
    pltpu.make_async_copy(dkv_ref, dkv_ref, g_recv.at[0]).wait()


def shards(key_value, key_gain, queries, tile_count, attn_gate, cotangent):
    n_rep = lax.axis_size("dp") * lax.axis_size("segment")
    vmem, anywhere = pl.BlockSpec(memory_space=pltpu.VMEM), pl.BlockSpec(memory_space=pl.ANY)
    dma = pltpu.SemaphoreType.DMA
    bf16, f32 = jnp.bfloat16, jnp.float32
    attended, d_key_value, d_gain, d_gate = pl.pallas_call(
        kernel,
        out_shape=(
            jax.ShapeDtypeStruct(queries.shape, bf16),
            jax.ShapeDtypeStruct(key_value.shape, bf16),
            jax.ShapeDtypeStruct((1, HEAD), f32),
            jax.ShapeDtypeStruct((1, HEAD), f32),
        ),
        in_specs=[anywhere, vmem, anywhere, vmem, pl.BlockSpec(memory_space=pltpu.SMEM), anywhere],
        out_specs=(anywhere, anywhere, vmem, vmem),
        scratch_shapes=[
            pltpu.VMEM((MICRO, OWN_KV, TILES, PATCH, WIDE), bf16),
            pltpu.VMEM((MICRO, OWN_HEADS, TEXT, HEAD), bf16),
            pltpu.VMEM((MICRO, OWN_HEADS, TEXT, HEAD), bf16),
            pltpu.VMEM((MICRO, OWN_KV, TILES, PATCH, WIDE), bf16),
            pltpu.VMEM((MICRO, OWN_HEADS, TEXT, HEAD), bf16),
            pltpu.VMEM((ROWS, GROUP * HEAD), bf16),
            pltpu.VMEM((ROWS, GROUP * HEAD), bf16),
            pltpu.VMEM((3, 8, HEAD), f32),
            pltpu.VMEM((SAMPLES, 8, HEAD), f32),
            pltpu.VMEM((TILES, 8, HEAD), f32),
            pltpu.VMEM((n_rep, 8, HEAD), f32),
            dma((MICRO, OWN_KV, TILES)), dma((MICRO, OWN_KV)),
            dma((MICRO, SAMPLES)), dma((MICRO, OWN_KV)),
            dma((MICRO, SAMPLES)), dma((MICRO, OWN_KV)),
            dma((MICRO, OWN_KV, TILES)), dma((1,)),
            dma((MICRO, OWN_HEADS)), dma((1,)),
            dma((SAMPLES,)), dma((1,)), dma((TILES,)), dma((1,)), dma((n_rep,)), dma((1,)),
        ],
        compiler_params=pltpu.CompilerParams(
            collective_id=0, has_side_effects=True, vmem_limit_bytes=48 * 1024 * 1024
        ),
        name="cross_attention",
    )(key_value, key_gain.reshape(1, HEAD), queries, tile_count, attn_gate, cotangent)
    return attended, d_key_value, d_gain.reshape(HEAD), d_gate[0, :1]


def solution(mesh):
    in_specs = (
        P("dp", ("segment", "mp"), None, None),
        P(),
        P("dp", "segment", None, "mp"),
        P("dp", "segment", None),
        P(),
        P("dp", "segment", None, "mp"),
    )
    out_specs = (P("dp", "segment", None, "mp"), P("dp", ("segment", "mp"), None, None), P(), P())
    return jax.shard_map(shards, mesh=mesh, in_specs=in_specs, out_specs=out_specs, check_vma=False)
```

time: 523 us -> 87.4 us (0.17)
  waiting for transfers between devices: 275 us -> 0 us
  blocking collectives: 109 us -> 0 us
  Pallas kernels: 0 us -> 77.5 us
  starting transfers between devices: 75.2 us -> 0 us
  local copies, waits for them, and re-layouts: 31.7 us -> 6.49 us
  other arithmetic: 14.2 us -> 0 us
  matrix products: 11.9 us -> 0 us
    all_to_all x4 -> x0, waiting for transfers between devices: 275 us -> none  [the longest x2 146 us: shards(): lax.all_to_all(outgoing, 'mp', split_axis=1, concat_axis=0, tiled=True)]
    psum x1 -> x0, blocking collectives: 109 us -> none  [shards(): d_gain, gate_total = lax.psum((d_gain, gate_total), ('segment', 'mp', 'dp'))]
    pallas_call x0 -> x1, Pallas kernels: none -> 77.5 us  [shards(): pl.pallas_call(kernel, out_shape=(jax.ShapeDtypeStruct(queries.shape, bf1...]
    all_to_all x4 -> x0, starting transfers between devices: 75.2 us -> none  [the longest x2 37.7 us: shards(): lax.all_to_all(back, 'mp', split_axis=0, concat_axis=1, tiled=True)[0]]
    slice x7 -> x0, local copies, waits for them, and re-layouts: 14.5 us -> none  [the longest x2 11.5 us: shards(): keys = kv_heads[:, :, :, 0]]
    dot_general x10 -> x0, matrix products: 11.9 us -> none  [the longest x2 5.98 us: shards(): jnp.einsum('skgtn,snkd->stkgd', probs_low, values, preferred_element_type...]
    reshape x4 -> x0, local copies, waits for them, and re-layouts: 7.67 us -> none  [the longest x2 7.52 us: shards(): kv_heads = arrived.reshape(samples, keys_all, kv_local, 2, HEAD)]
  transfers between devices with their start and end apart: 4 -> 0, of which waited for: 4 -> 0; matrix products, arithmetic and copies ran while one was open for 8% -> 0% of each run, Pallas kernels for 0% -> 0%
where the time goes in v1:
time: 87.4 us; the launch traced here: 86.4 us
  Pallas kernels  77.5 us (89%)
  local copies, waits for them, and re-layouts  6.49 us (7%)
  between operations  2.47 us (3%)
    pallas_call x1, Pallas kernels, shards(): pl.pallas_call(kernel, out_shape=(jax.ShapeDtypeStruct(queries.shape, bf1...  77.5 us
    unnamed x13, local copies, waits for them, and re-layouts  6.49 us

profile of v1, /device:TPU:1, one launch (start us, length us, event | category | flops | bytes accessed | tf_op | source)
XLA Modules:
  0.0 86.4 jit_solution(14817258618920504153)
XLA Ops:
  1.3 0.0 copy-start.4
  1.3 0.6 copy-done.4
  1.9 0.0 copy-start
  1.9 1.1 %copy-done = bf16[2,1,96,2048]{3,2,1,0:T(8,128)(2,1)S(1)} copy-done((bf16[2,1,96,2048]{3,2,1,0:T(8,128)(2,1)S(1)}, bf16[2,1,96,2048]{3,2,1,0:T(8,128)(2,1)}, u32[]{:S(2)}) %copy-start) | copy-done | bytes 786456
  3.1 0.0 copy-start.1
  3.1 0.9 %copy-done.1 = bf16[2,16,32,128]{3,2,1,0:T(8,128)(2,1)S(1)} copy-done((bf16[2,16,32,128]{3,2,1,0:T(8,128)(2,1)S(1)}, bf16[2,16,32,128]{3,2,1,0:T(8,128)(2,1)}, u32[]{:S(2)}) %copy-start.1) | copy-done | bytes 262168
  4.0 0.0 copy-start.2
  4.0 0.9 %copy-done.2 = bf16[2,16,32,128]{3,2,1,0:T(8,128)(2,1)S(1)} copy-done((bf16[2,16,32,128]{3,2,1,0:T(8,128)(2,1)S(1)}, bf16[2,16,32,128]{3,2,1,0:T(8,128)(2,1)}, u32[]{:S(2)}) %copy-start.2) | copy-done | bytes 262168
  5.0 0.0 copy-start.3
  5.0 0.7 copy-done.3
  5.7 77.5 %cross_attention.1 = (bf16[2,16,32,128]{3,2,1,0:T(8,128)(2,1)S(1)}, bf16[2,1,96,2048]{3,2,1,0:T(8,128)(2,1)S(1)}, f32[1,128]{1,0:T(1,128)S(1)}, f32[1,128]{1,0:T(1,128)S(1)}) custom-call(bf16[2,1,96,2048]{3,2,1,0:T(8,128)(2,1)S(1)} %copy-done, f32[1,128]{1,0:T(1,128)S(1)} %bitcast.4, bf16[2,16,32,128]{3,2,1,0:T(8,128)(2,1)S(1)} %copy-done.1, ...), custom_call_target="tpu_custom_call" | custom-call | tf_op jit(solution)/shard_map/cross_attention/pallas_call | solution.py:367
  83.2 0.7 copy.15
  83.9 0.9 %copy.16 = bf16[2,1,96,2048]{3,2,1,0:T(8,128)(2,1)} copy(bf16[2,1,96,2048]{3,2,1,0:T(8,128)(2,1)S(1)} %get-tuple-element.17) | data formatting | bytes 1572864
  84.8 0.5 copy.17
Async XLA Ops:
  1.3 0.7 copy-start.4
  1.9 1.1 %copy-start = (bf16[2,1,96,2048]{3,2,1,0:T(8,128)(2,1)S(1)}, bf16[2,1,96,2048]{3,2,1,0:T(8,128)(2,1)}, u32[]{:S(2)}) copy-start(bf16[2,1,96,2048]{3,2,1,0:T(8,128)(2,1)} %kv_ref.1) | copy-start | bytes 2359300
  3.1 0.9 %copy-start.1 = (bf16[2,16,32,128]{3,2,1,0:T(8,128)(2,1)S(1)}, bf16[2,16,32,128]{3,2,1,0:T(8,128)(2,1)}, u32[]{:S(2)}) copy-start(bf16[2,16,32,128]{3,2,1,0:T(8,128)(2,1)} %q_ref.1) | copy-start | bytes 786436
  4.0 0.9 %copy-start.2 = (bf16[2,16,32,128]{3,2,1,0:T(8,128)(2,1)S(1)}, bf16[2,16,32,128]{3,2,1,0:T(8,128)(2,1)}, u32[]{:S(2)}) copy-start(bf16[2,16,32,128]{3,2,1,0:T(8,128)(2,1)} %cot_ref.1) | copy-start | bytes 786436
  5.0 0.7 copy-start.3

commit v2 on v1

--- a/solution.py
+++ b/solution.py
@@ -17,6 +17,8 @@
 OWN_HEADS = OWN_KV * GROUP
 ROWS = GROUP * TEXT
 WIDE = 2 * HEAD
+GRADS_AT_ONCE = 1
+GRADS_AFTER = ((1,), (2,), (3,))
 SCALE = 1.0 / HEAD**0.5
 
 
@@ -30,6 +32,7 @@
     kvbuf, qbuf, cbuf, gbuf, abuf, qblk, dblk, red_src, red1, red2, red3,
     kv_send, kv_recv, q_send, q_recv, c_send, c_recv, g_send, g_recv, a_send, a_recv,
     r1_send, r1_recv, r2_send, r2_recv, r3_send, r3_recv,
+    gain_v, count_v, small_sem,
 ):
     me = lax.axis_index("mp")
     seg = lax.axis_index("segment")
@@ -56,8 +59,23 @@
     def member_part(i):
         return (i + TILES - (sample // 2) % TILES) % TILES
 
+    def turn(k):
+        r = k // 2
+        row = sample // 2 + 8 + ((r + 1) // 2) * (1 - 2 * (r % 2))
+        return (row % 8) * 2 + (k + sample) % 2
+
+    def other(k):
+        return (place + 1 + k) % TILES
+
     def rep_id(i):
         return {"segment": i % lax.axis_size("segment"), "dp": i // lax.axis_size("segment")}
+
+    smalls = [
+        pltpu.make_async_copy(gain_ref, gain_v, small_sem.at[0]),
+        pltpu.make_async_copy(count_ref, count_v, small_sem.at[1]),
+    ]
+    for copy in smalls:
+        copy.start()
 
     barrier = pltpu.get_barrier_semaphore()
     has_self = (part == my_part).astype(jnp.int32)
@@ -113,18 +131,18 @@
         )
 
     def send_kv(b, u):
-        def step(i, _):
-            @pl.when(i != place)
-            def _():
-                kv_copy(b, u, i).start()
+        def step(k, _):
+            kv_copy(b, u, other(k)).start()
             return 0
-        lax.fori_loop(0, TILES, step, 0)
+        lax.fori_loop(0, TILES - 1, step, 0)
         pltpu.make_async_copy(
             kv_ref.at[b, 0, :, columns(part, u)], kvbuf.at[b, u, place], kv_recv.at[b, u]
         ).start()
 
     def send_heads(b):
-        def q_step(n, _):
+        def q_step(k, _):
+            n = turn(k)
+
             @pl.when(worker(n) != me)
             def _():
                 q_copy(b, n).start()
@@ -134,7 +152,9 @@
                 pltpu.make_async_copy(q_ref.at[b, n], qbuf.at[b, my_slot], q_recv.at[b, my_unit]).start()
             return 0
 
-        def c_step(n, _):
+        def c_step(k, _):
+            n = turn(k)
+
             @pl.when(worker(n) != me)
             def _():
                 c_copy(b, n).start()
@@ -152,8 +172,10 @@
         send_heads(b)
         send_kv(b, 1)
 
+    for copy in smalls:
+        copy.wait()
     gate = jnp.tanh(jnp.full((1, HEAD), gate_ref[0], jnp.float32))
-    gain = gain_ref[...]
+    gain = gain_v[...]
     token_of = (lax.broadcasted_iota(jnp.int32, (ROWS, TEXT), 0) & (TEXT - 1)) == (
         lax.broadcasted_iota(jnp.int32, (ROWS, TEXT), 1)
     )
@@ -171,6 +193,31 @@
             abuf.at[b, i], att_ref.at[b, sample], a_send.at[b, i], a_recv.at[0],
             device_id={"mp": owner(i)},
         )
+
+    def send_grads(b, u):
+        def g_step(k, _):
+            g_copy(b, u, other(k)).start()
+            return 0
+
+        lax.fori_loop(0, TILES - 1, g_step, 0)
+        pltpu.make_async_copy(
+            gbuf.at[b, u, place], dkv_ref.at[b, 0, :, columns(part, u)], g_recv.at[0]
+        ).start()
+
+    def send_attended(b, u):
+        def a_step(k, _):
+            i = u * GROUP + (k + me) % GROUP
+
+            @pl.when(owner(i) != me)
+            def _():
+                a_copy(b, i).start()
+
+            @pl.when(owner(i) == me)
+            def _():
+                pltpu.make_async_copy(abuf.at[b, i], att_ref.at[b, sample], a_recv.at[0]).start()
+            return 0
+
+        lax.fori_loop(0, GROUP, a_step, 0)
 
     def unit(step, carry):
         gain_sum, gate_sum = carry
@@ -178,7 +225,7 @@
         u = step % OWN_KV
         heads = pl.ds(u * GROUP, GROUP)
         q_view, c_view = qbuf.at[b, heads], cbuf.at[b, heads]
-        counts = count_ref[b, pl.ds(sample, 1), :].astype(jnp.float32).astype(jnp.bfloat16)
+        counts = count_v[b, pl.ds(sample, 1), :].astype(jnp.float32).astype(jnp.bfloat16)
         count_col = dot(spread, jnp.broadcast_to(counts, (HEAD, TEXT)), ((1,), (1,)))
         count_row = dot(jnp.broadcast_to(counts, (8, TEXT)), spread, ((1,), (1,)))[0:1]
         live = (count_col > 0.5).astype(jnp.float32)
@@ -203,19 +250,7 @@
         mixed = dot(probs_low, values, ((0,), (0,)))
         abuf[b, heads] = (gate_live * mixed).astype(jnp.bfloat16).reshape(GROUP, TEXT, HEAD)
 
-        def a_step(k, _):
-            i = u * GROUP + k
-
-            @pl.when(owner(i) != me)
-            def _():
-                a_copy(b, i).start()
-
-            @pl.when(owner(i) == me)
-            def _():
-                pltpu.make_async_copy(abuf.at[b, i], att_ref.at[b, sample], a_recv.at[0]).start()
-            return 0
-
-        lax.fori_loop(0, GROUP, a_step, 0)
+        send_attended(b, u)
 
         pltpu.make_async_copy(c_view, c_view, c_recv.at[b, u]).wait()
         cotan = c_view[...].reshape(ROWS, HEAD).astype(jnp.float32)
@@ -245,16 +280,11 @@
         gbuf[b, u, :, :, :HEAD] = d_key.astype(jnp.bfloat16).reshape(TILES, PATCH, HEAD)
         gbuf[b, u, :, :, HEAD:] = value_part.reshape(TILES, PATCH, HEAD)
 
-        def g_step(i, _):
-            @pl.when(i != place)
-            def _():
-                g_copy(b, u, i).start()
-            return 0
-
-        lax.fori_loop(0, TILES, g_step, 0)
-        pltpu.make_async_copy(
-            gbuf.at[b, u, place], dkv_ref.at[b, 0, :, columns(part, u)], g_recv.at[0]
-        ).start()
+
+        @pl.when(step < GRADS_AT_ONCE)
+        def _():
+            send_grads(b, u)
+
         return gain_sum, gate_sum
 
     zero = jnp.zeros((1, HEAD), jnp.float32)
@@ -272,7 +302,9 @@
             red_src.at[0], red1.at[my_slot], r1_send.at[n], r1_recv.at[0], device_id={"mp": worker(n)}
         )
 
-    def r1_step(n, _):
+    def r1_step(k, _):
+        n = turn(k)
+
         @pl.when(worker(n) != me)
         def _():
             r1_copy(n).start()
@@ -283,6 +315,8 @@
         return 0
 
     lax.fori_loop(0, SAMPLES, r1_step, 0)
+    for step in GRADS_AFTER[0]:
+        send_grads(step // OWN_KV, step % OWN_KV)
     pltpu.make_async_copy(red1, red1, r1_recv.at[0]).wait()
     red_src[1] = jnp.sum(red1[...], axis=0)
 
@@ -291,14 +325,14 @@
             red_src.at[1], red2.at[place], r2_send.at[i], r2_recv.at[0], device_id={"mp": member(i)}
         )
 
-    def r2_step(i, _):
-        @pl.when(i != place)
-        def _():
-            r2_copy(i).start()
-        return 0
-
-    lax.fori_loop(0, TILES, r2_step, 0)
+    def r2_step(k, _):
+        r2_copy(other(k)).start()
+        return 0
+
+    lax.fori_loop(0, TILES - 1, r2_step, 0)
     pltpu.make_async_copy(red_src.at[1], red2.at[place], r2_recv.at[0]).start()
+    for step in GRADS_AFTER[1]:
+        send_grads(step // OWN_KV, step % OWN_KV)
     pltpu.make_async_copy(red2, red2, r2_recv.at[0]).wait()
     red_src[2] = jnp.sum(red2[...], axis=0)
 
@@ -315,6 +349,9 @@
 
     lax.fori_loop(0, n_rep, r3_step, 0)
     pltpu.make_async_copy(red_src.at[2], red3.at[rep], r3_recv.at[0]).start()
+
+    for step in GRADS_AFTER[2]:
+        send_grads(step // OWN_KV, step % OWN_KV)
 
     def heads_sent(n, _):
         @pl.when(worker(n) != me)
@@ -353,7 +390,7 @@
     pltpu.make_async_copy(red3, red3, r3_recv.at[0]).wait()
     total = jnp.sum(red3[...], axis=0)
     dgain_ref[...] = total[0:1]
-    dgate_ref[...] = jnp.sum(total[1:2], axis=1, keepdims=True) * (1.0 - gate * gate)
+    dgate_ref[...] = jnp.broadcast_to(jnp.sum(total[1:2], axis=1, keepdims=True) * (1.0 - gate * gate), (1, HEAD))
 
     pltpu.make_async_copy(att_ref, att_ref, a_recv.at[0]).wait()
     pltpu.make_async_copy(dkv_ref, dkv_ref, g_recv.at[0]).wait()
@@ -362,8 +399,14 @@
 def shards(key_value, key_gain, queries, tile_count, attn_gate, cotangent):
     n_rep = lax.axis_size("dp") * lax.axis_size("segment")
     vmem, anywhere = pl.BlockSpec(memory_space=pltpu.VMEM), pl.BlockSpec(memory_space=pl.ANY)
+    hbm = pl.BlockSpec(memory_space=pltpu.HBM)
     dma = pltpu.SemaphoreType.DMA
     bf16, f32 = jnp.bfloat16, jnp.float32
+    gain_row = key_gain.reshape(1, HEAD)
+    key_value, gain_row, queries, tile_count, cotangent = (
+        pltpu.with_memory_space_constraint(x, pltpu.HBM)
+        for x in (key_value, gain_row, queries, tile_count, cotangent)
+    )
     attended, d_key_value, d_gain, d_gate = pl.pallas_call(
         kernel,
         out_shape=(
@@ -372,7 +415,7 @@
             jax.ShapeDtypeStruct((1, HEAD), f32),
             jax.ShapeDtypeStruct((1, HEAD), f32),
         ),
-        in_specs=[anywhere, vmem, anywhere, vmem, pl.BlockSpec(memory_space=pltpu.SMEM), anywhere],
+        in_specs=[hbm, hbm, hbm, hbm, pl.BlockSpec(memory_space=pltpu.SMEM), hbm],
         out_specs=(anywhere, anywhere, vmem, vmem),
         scratch_shapes=[
             pltpu.VMEM((MICRO, OWN_KV, TILES, PATCH, WIDE), bf16),
@@ -392,12 +435,13 @@
             dma((MICRO, OWN_KV, TILES)), dma((1,)),
             dma((MICRO, OWN_HEADS)), dma((1,)),
             dma((SAMPLES,)), dma((1,)), dma((TILES,)), dma((1,)), dma((n_rep,)), dma((1,)),
+            pltpu.VMEM((1, HEAD), f32), pltpu.VMEM(tile_count.shape, jnp.int32), dma((2,)),
         ],
         compiler_params=pltpu.CompilerParams(
             collective_id=0, has_side_effects=True, vmem_limit_bytes=48 * 1024 * 1024
         ),
         name="cross_attention",
-    )(key_value, key_gain.reshape(1, HEAD), queries, tile_count, attn_gate, cotangent)
+    )(key_value, gain_row, queries, tile_count, attn_gate, cotangent)
     return attended, d_key_value, d_gain.reshape(HEAD), d_gate[0, :1]
 
 

time: 87.4 us -> 76 us (0.87); the launches traced: 86.4 us -> 75.9 us
  Pallas kernels: 77.5 us -> 71.4 us
  local copies, waits for them, and re-layouts: 6.49 us -> 2.1 us
    pallas_call x1, Pallas kernels: 77.5 us -> 71.4 us  [shards(): pl.pallas_call(kernel, out_shape=(jax.ShapeDtypeStruct(queries.shape, bf1...]
    unnamed x13 -> x3, local copies, waits for them, and re-layouts: 6.49 us -> 2.1 us
where the time goes in v2:
time: 76 us; the launch traced here: 75.9 us
  Pallas kernels  71.4 us (94%)
  between operations  2.45 us (3%)
  local copies, waits for them, and re-layouts  2.1 us (3%)
    pallas_call x1, Pallas kernels, shards(): pl.pallas_call(kernel, out_shape=(jax.ShapeDtypeStruct(queries.shape, bf1...  71.4 us
    unnamed x3, local copies, waits for them, and re-layouts  2.1 us

profile of v2, /device:TPU:1, one launch (start us, length us, event | category | flops | bytes accessed | tf_op | source)
XLA Modules:
  0.0 75.9 jit_solution(3068360716097283287)
XLA Ops:
  1.3 71.4 %cross_attention.1 = (bf16[2,16,32,128]{3,2,1,0:T(8,128)(2,1)S(1)}, bf16[2,1,96,2048]{3,2,1,0:T(8,128)(2,1)S(1)}, f32[1,128]{1,0:T(1,128)S(1)}, f32[1,128]{1,0:T(1,128)S(1)}) custom-call(bf16[2,1,96,2048]{3,2,1,0:T(8,128)(2,1)} %kv_ref.1, f32[1,128]{1,0:T(1,128)} %bitcast.6, bf16[2,16,32,128]{3,2,1,0:T(8,128)(2,1)} %q_ref.1, s32[2,16,32]{2,1,0:T(8,128)} %count_ref.1, ...), custom_call_target="tpu_custom_call" | custom-call | tf_op jit(solution)/shard_map/cross_attention/pallas_call | solution.py:410
  72.6 0.7 copy.15
  73.4 0.9 %copy.16 = bf16[2,1,96,2048]{3,2,1,0:T(8,128)(2,1)} copy(bf16[2,1,96,2048]{3,2,1,0:T(8,128)(2,1)S(1)} %get-tuple-element.17) | data formatting | bytes 1572864
  74.2 0.5 copy.17

commit v3 on v2

--- a/solution.py
+++ b/solution.py
@@ -18,7 +18,12 @@
 ROWS = GROUP * TEXT
 WIDE = 2 * HEAD
 GRADS_AT_ONCE = 1
-GRADS_AFTER = ((1,), (2,), (3,))
+GRADS_AFTER = ((1,), (2, 3))
+ORDER = (
+    (((0, 0), (0, 1), (1, 0)), (), ((1, 1),)),
+    (((0, 0),), (), ((0, 1), (1, 0), (1, 1))),
+)
+HOLD_A = 1
 SCALE = 1.0 / HEAD**0.5
 
 
@@ -29,16 +34,16 @@
 def kernel(
     kv_ref, gain_ref, q_ref, count_ref, gate_ref, cot_ref,
     att_ref, dkv_ref, dgain_ref, dgate_ref,
-    kvbuf, qbuf, cbuf, gbuf, abuf, qblk, dblk, red_src, red1, red2, red3,
+    kvbuf, qbuf, cbuf, gbuf, abuf, qblk, dblk, red_src, red_rep, red_plane,
     kv_send, kv_recv, q_send, q_recv, c_send, c_recv, g_send, g_recv, a_send, a_recv,
-    r1_send, r1_recv, r2_send, r2_recv, r3_send, r3_recv,
-    gain_v, count_v, small_sem,
+    rep_send, plane_send, sum_recv,
+    gain_v, count_v, small_sem, go_sem, all_sem, rep_sem,
 ):
     me = lax.axis_index("mp")
     seg = lax.axis_index("segment")
     dp = lax.axis_index("dp")
-    n_dp = lax.axis_size("dp")
-    n_rep = n_dp * lax.axis_size("segment")
+    n_mp = lax.axis_size("mp")
+    n_rep = lax.axis_size("dp") * lax.axis_size("segment")
     sample = me // TILES
     place = me % TILES
     part = (place + TILES - (sample // 2) % TILES) % TILES
@@ -78,36 +83,63 @@
         copy.start()
 
     barrier = pltpu.get_barrier_semaphore()
-    has_self = (part == my_part).astype(jnp.int32)
-
-    def greet_heads(i, _):
-        @pl.when(worker(i) != me)
-        def _():
-            pl.semaphore_signal(barrier, inc=1, device_id={"mp": worker(i)})
-
-        @pl.when(owner(i) != me)
-        def _():
-            pl.semaphore_signal(barrier, inc=1, device_id={"mp": owner(i)})
-        return 0
-
-    def greet_members(i, _):
-        @pl.when(i != place)
-        def _():
-            pl.semaphore_signal(barrier, inc=1, device_id={"mp": member(i)})
-        return 0
-
-    def greet_reps(i, _):
-        @pl.when(i != rep)
-        def _():
-            pl.semaphore_signal(barrier, inc=1, device_id=rep_id(i))
-        return 0
-
-    lax.fori_loop(0, TILES, greet_members, 0)
-    lax.fori_loop(0, SAMPLES, greet_heads, 0)
-    lax.fori_loop(0, n_rep, greet_reps, 0)
-    qblk[...] = jnp.zeros_like(qblk)
-    dblk[...] = jnp.zeros_like(dblk)
-    pl.semaphore_wait(barrier, 2 * (SAMPLES - has_self) + TILES - 1 + n_rep - 1)
+
+    def tell(sem, first):
+        def step(k, _):
+            pl.semaphore_signal(sem, inc=1, device_id={"mp": member((first + 1 + k) % TILES)})
+            return 0
+        lax.fori_loop(0, TILES - 1, step, 0)
+
+    @pl.when(place == 0)
+    def _():
+        pl.semaphore_wait(barrier, TILES - 1)
+        tell(go_sem, 0)
+
+    @pl.when(place != 0)
+    def _():
+        pl.semaphore_signal(barrier, inc=1, device_id={"mp": member(0)})
+        pl.semaphore_wait(go_sem, 1)
+
+    def greet_samples(k, _):
+        n = place * TILES + k
+
+        @pl.when(n != sample)
+        def _():
+            pl.semaphore_signal(barrier, inc=1, device_id={"mp": n * TILES + 1})
+        return 0
+
+    lax.fori_loop(0, SAMPLES // TILES, greet_samples, 0)
+
+    def wait_plane():
+        @pl.when(place == 1)
+        def _():
+            pl.semaphore_wait(barrier, SAMPLES - 1)
+            tell(all_sem, 1)
+
+        @pl.when(place != 1)
+        def _():
+            pl.semaphore_wait(all_sem, 1)
+
+    def greet_reps():
+        def step(i, _):
+            @pl.when(i != rep)
+            def _():
+                pl.semaphore_signal(barrier, inc=1, device_id=rep_id(i))
+            return 0
+
+        @pl.when(place == 2)
+        def _():
+            lax.fori_loop(0, n_rep, step, 0)
+
+    def wait_reps():
+        @pl.when(place == 2)
+        def _():
+            pl.semaphore_wait(barrier, n_rep - 1)
+            tell(rep_sem, 2)
+
+        @pl.when(place != 2)
+        def _():
+            pl.semaphore_wait(rep_sem, 1)
 
     def columns(p, u):
         return pl.ds(pl.multiple_of((p * OWN_KV + u) * WIDE, WIDE), WIDE)
@@ -167,10 +199,26 @@
         lax.fori_loop(0, SAMPLES, q_step, 0)
         lax.fori_loop(0, SAMPLES, c_step, 0)
 
-    for b in range(MICRO):
-        send_kv(b, 0)
-        send_heads(b)
-        send_kv(b, 1)
+    def send_units(units, when):
+        @pl.when(when)
+        def _():
+            for b, u in units:
+                send_kv(b, u)
+
+    first_half = sample % 2 == 0
+    for half, when in ((0, first_half), (1, jnp.logical_not(first_half))):
+        send_units(ORDER[half][0], when)
+    qblk[...] = jnp.zeros_like(qblk)
+    dblk[...] = jnp.zeros_like(dblk)
+    wait_plane()
+    greet_reps()
+    send_heads(0)
+    for half, when in ((0, first_half), (1, jnp.logical_not(first_half))):
+        send_units(ORDER[half][1], when)
+    send_heads(1)
+    for half, when in ((0, first_half), (1, jnp.logical_not(first_half))):
+        send_units(ORDER[half][2], when)
+    wait_reps()
 
     for copy in smalls:
         copy.wait()
@@ -250,7 +298,9 @@
         mixed = dot(probs_low, values, ((0,), (0,)))
         abuf[b, heads] = (gate_live * mixed).astype(jnp.bfloat16).reshape(GROUP, TEXT, HEAD)
 
-        send_attended(b, u)
+        @pl.when(step < MICRO * OWN_KV - HOLD_A)
+        def _():
+            send_attended(b, u)
 
         pltpu.make_async_copy(c_view, c_view, c_recv.at[b, u]).wait()
         cotan = c_view[...].reshape(ROWS, HEAD).astype(jnp.float32)
@@ -290,68 +340,43 @@
     zero = jnp.zeros((1, HEAD), jnp.float32)
     gain_sum, gate_sum = lax.fori_loop(0, MICRO * OWN_KV, unit, (zero, zero))
 
-    row = lax.broadcasted_iota(jnp.int32, (8, HEAD), 0)
-
-    def spread_sums(gain_sum, gate_sum):
-        return jnp.where(row == 0, gain_sum, jnp.where(row == 1, gate_sum, 0.0))
-
-    red_src[0] = spread_sums(gain_sum, gate_sum)
-
-    def r1_copy(n):
-        return pltpu.make_async_remote_copy(
-            red_src.at[0], red1.at[my_slot], r1_send.at[n], r1_recv.at[0], device_id={"mp": worker(n)}
-        )
-
-    def r1_step(k, _):
-        n = turn(k)
-
-        @pl.when(worker(n) != me)
-        def _():
-            r1_copy(n).start()
-
-        @pl.when(worker(n) == me)
-        def _():
-            pltpu.make_async_copy(red_src.at[0], red1.at[my_slot], r1_recv.at[0]).start()
-        return 0
-
-    lax.fori_loop(0, SAMPLES, r1_step, 0)
-    for step in GRADS_AFTER[0]:
-        send_grads(step // OWN_KV, step % OWN_KV)
-    pltpu.make_async_copy(red1, red1, r1_recv.at[0]).wait()
-    red_src[1] = jnp.sum(red1[...], axis=0)
-
-    def r2_copy(i):
-        return pltpu.make_async_remote_copy(
-            red_src.at[1], red2.at[place], r2_send.at[i], r2_recv.at[0], device_id={"mp": member(i)}
-        )
-
-    def r2_step(k, _):
-        r2_copy(other(k)).start()
-        return 0
-
-    lax.fori_loop(0, TILES - 1, r2_step, 0)
-    pltpu.make_async_copy(red_src.at[1], red2.at[place], r2_recv.at[0]).start()
-    for step in GRADS_AFTER[1]:
-        send_grads(step // OWN_KV, step % OWN_KV)
-    pltpu.make_async_copy(red2, red2, r2_recv.at[0]).wait()
-    red_src[2] = jnp.sum(red2[...], axis=0)
-
-    def r3_copy(i):
-        return pltpu.make_async_remote_copy(
-            red_src.at[2], red3.at[rep], r3_send.at[i], r3_recv.at[0], device_id=rep_id(i)
-        )
-
-    def r3_step(i, _):
-        @pl.when(i != rep)
-        def _():
-            r3_copy(i).start()
-        return 0
-
-    lax.fori_loop(0, n_rep, r3_step, 0)
-    pltpu.make_async_copy(red_src.at[2], red3.at[rep], r3_recv.at[0]).start()
-
-    for step in GRADS_AFTER[2]:
-        send_grads(step // OWN_KV, step % OWN_KV)
+    red_src[0, 0:1] = gain_sum
+    red_src[0, 1:2] = gate_sum
+
+    def after_sums(i):
+        for step in GRADS_AFTER[i]:
+            send_grads(step // OWN_KV, step % OWN_KV)
+
+    def rep_copy(k):
+        return pltpu.make_async_remote_copy(
+            red_src.at[0], red_rep.at[rep], rep_send.at[k], sum_recv.at[0], device_id=rep_id(k)
+        )
+
+    def plane_copy(k):
+        return pltpu.make_async_remote_copy(
+            red_src.at[1], red_plane.at[me], plane_send.at[k], sum_recv.at[1], device_id={"mp": (me + k) % n_mp}
+        )
+
+    def rep_step(k, _):
+        @pl.when(k != rep)
+        def _():
+            rep_copy(k).start()
+        return 0
+
+    def plane_step(k, _):
+        plane_copy(k).start()
+        return 0
+
+    lax.fori_loop(0, n_rep, rep_step, 0)
+    pltpu.make_async_copy(red_src.at[0], red_rep.at[rep], sum_recv.at[0]).start()
+    for step in range(MICRO * OWN_KV - HOLD_A, MICRO * OWN_KV):
+        send_attended(step // OWN_KV, step % OWN_KV)
+    after_sums(0)
+    pltpu.make_async_copy(red_rep, red_rep, sum_recv.at[0]).wait()
+    red_src[1] = jnp.sum(red_rep[...], axis=0)
+    pltpu.make_async_copy(red_src.at[1], red_plane.at[me], sum_recv.at[1]).start()
+    lax.fori_loop(1, n_mp, plane_step, 0)
+    after_sums(1)
 
     def heads_sent(n, _):
         @pl.when(worker(n) != me)
@@ -359,7 +384,6 @@
             for b in range(MICRO):
                 q_copy(b, n).wait_send()
                 c_copy(b, n).wait_send()
-            r1_copy(n).wait_send()
 
         @pl.when(owner(n) != me)
         def _():
@@ -374,21 +398,25 @@
                 for u in range(OWN_KV):
                     kv_copy(b, u, i).wait_send()
                     g_copy(b, u, i).wait_send()
-            r2_copy(i).wait_send()
-        return 0
-
-    def reps_sent(i, _):
-        @pl.when(i != rep)
-        def _():
-            r3_copy(i).wait_send()
+        return 0
+
+    def reps_sent(k, _):
+        @pl.when(k != rep)
+        def _():
+            rep_copy(k).wait_send()
+        return 0
+
+    def plane_sent(k, _):
+        plane_copy(k).wait_send()
         return 0
 
     lax.fori_loop(0, SAMPLES, heads_sent, 0)
     lax.fori_loop(0, TILES, members_sent, 0)
     lax.fori_loop(0, n_rep, reps_sent, 0)
-
-    pltpu.make_async_copy(red3, red3, r3_recv.at[0]).wait()
-    total = jnp.sum(red3[...], axis=0)
+    lax.fori_loop(1, n_mp, plane_sent, 0)
+
+    pltpu.make_async_copy(red_plane, red_plane, sum_recv.at[1]).wait()
+    total = jnp.sum(red_plane[...], axis=0)
     dgain_ref[...] = total[0:1]
     dgate_ref[...] = jnp.broadcast_to(jnp.sum(total[1:2], axis=1, keepdims=True) * (1.0 - gate * gate), (1, HEAD))
 
@@ -398,6 +426,7 @@
 
 def shards(key_value, key_gain, queries, tile_count, attn_gate, cotangent):
     n_rep = lax.axis_size("dp") * lax.axis_size("segment")
+    n_mp = lax.axis_size("mp")
     vmem, anywhere = pl.BlockSpec(memory_space=pltpu.VMEM), pl.BlockSpec(memory_space=pl.ANY)
     hbm = pl.BlockSpec(memory_space=pltpu.HBM)
     dma = pltpu.SemaphoreType.DMA
@@ -425,17 +454,17 @@
             pltpu.VMEM((MICRO, OWN_HEADS, TEXT, HEAD), bf16),
             pltpu.VMEM((ROWS, GROUP * HEAD), bf16),
             pltpu.VMEM((ROWS, GROUP * HEAD), bf16),
-            pltpu.VMEM((3, 8, HEAD), f32),
-            pltpu.VMEM((SAMPLES, 8, HEAD), f32),
-            pltpu.VMEM((TILES, 8, HEAD), f32),
-            pltpu.VMEM((n_rep, 8, HEAD), f32),
+            pltpu.VMEM((2, 2, HEAD), f32),
+            pltpu.VMEM((n_rep, 2, HEAD), f32),
+            pltpu.VMEM((n_mp, 2, HEAD), f32),
             dma((MICRO, OWN_KV, TILES)), dma((MICRO, OWN_KV)),
             dma((MICRO, SAMPLES)), dma((MICRO, OWN_KV)),
             dma((MICRO, SAMPLES)), dma((MICRO, OWN_KV)),
             dma((MICRO, OWN_KV, TILES)), dma((1,)),
             dma((MICRO, OWN_HEADS)), dma((1,)),
-            dma((SAMPLES,)), dma((1,)), dma((TILES,)), dma((1,)), dma((n_rep,)), dma((1,)),
+            dma((n_rep,)), dma((n_mp,)), dma((2,)),
             pltpu.VMEM((1, HEAD), f32), pltpu.VMEM(tile_count.shape, jnp.int32), dma((2,)),
+            pltpu.SemaphoreType.REGULAR, pltpu.SemaphoreType.REGULAR, pltpu.SemaphoreType.REGULAR,
         ],
         compiler_params=pltpu.CompilerParams(
             collective_id=0, has_side_effects=True, vmem_limit_bytes=48 * 1024 * 1024

time: 76 us -> 72.2 us (0.950)
  Pallas kernels: 71.4 us -> 67.5 us
    pallas_call x1, Pallas kernels: 71.4 us -> 67.5 us  [shards(): pl.pallas_call(kernel, out_shape=(jax.ShapeDtypeStruct(queries.shape, bf1...]
where the time goes in v3:
time: 72.2 us; the launch traced here: 72 us
  Pallas kernels  67.5 us (93%)
  between operations  2.45 us (3%)
  local copies, waits for them, and re-layouts  2.1 us (3%)
    pallas_call x1, Pallas kernels, shards(): pl.pallas_call(kernel, out_shape=(jax.ShapeDtypeStruct(queries.shape, bf1...  67.5 us
    unnamed x3, local copies, waits for them, and re-layouts  2.1 us

profile of v3, /device:TPU:1, one launch (start us, length us, event | category | flops | bytes accessed | tf_op | source)
XLA Modules:
  0.0 72.0 jit_solution(6728195961413223656)
XLA Ops:
  1.3 67.5 %cross_attention.1 = (bf16[2,16,32,128]{3,2,1,0:T(8,128)(2,1)S(1)}, bf16[2,1,96,2048]{3,2,1,0:T(8,128)(2,1)S(1)}, f32[1,128]{1,0:T(1,128)S(1)}, f32[1,128]{1,0:T(1,128)S(1)}) custom-call(bf16[2,1,96,2048]{3,2,1,0:T(8,128)(2,1)} %kv_ref.1, f32[1,128]{1,0:T(1,128)} %bitcast.6, bf16[2,16,32,128]{3,2,1,0:T(8,128)(2,1)} %q_ref.1, s32[2,16,32]{2,1,0:T(8,128)} %count_ref.1, ...), custom_call_target="tpu_custom_call" | custom-call | tf_op jit(solution)/shard_map/cross_attention/pallas_call | solution.py:439
  68.8 0.7 copy.15
  69.5 0.9 %copy.16 = bf16[2,1,96,2048]{3,2,1,0:T(8,128)(2,1)} copy(bf16[2,1,96,2048]{3,2,1,0:T(8,128)(2,1)S(1)} %get-tuple-element.17) | data formatting | bytes 1572864
  70.4 0.5 copy.17

commit v4 on v3

--- a/solution.py
+++ b/solution.py
@@ -20,8 +20,8 @@
 GRADS_AT_ONCE = 1
 GRADS_AFTER = ((1,), (2, 3))
 ORDER = (
-    (((0, 0), (0, 1), (1, 0)), (), ((1, 1),)),
-    (((0, 0),), (), ((0, 1), (1, 0), (1, 1))),
+    (((0, 0), (0, 1)), ((1, 0),), ((1, 1),)),
+    (((0, 0),), ((0, 1),), ((1, 0), (1, 1))),
 )
 HOLD_A = 1
 SCALE = 1.0 / HEAD**0.5
@@ -267,6 +267,28 @@
 
         lax.fori_loop(0, GROUP, a_step, 0)
 
+    def rep_copy(k):
+        return pltpu.make_async_remote_copy(
+            red_src.at[0], red_rep.at[rep], rep_send.at[k], sum_recv.at[0], device_id=rep_id(k)
+        )
+
+    def plane_copy(k):
+        return pltpu.make_async_remote_copy(
+            red_src.at[1], red_plane.at[me], plane_send.at[k], sum_recv.at[1], device_id={"mp": (me + k) % n_mp}
+        )
+
+    def rep_step(k, _):
+        @pl.when(k != rep)
+        def _():
+            rep_copy(k).start()
+        return 0
+
+    def send_sums(gain_sum, gate_sum):
+        red_src[0, 0:1] = gain_sum
+        red_src[0, 1:2] = gate_sum
+        lax.fori_loop(0, n_rep, rep_step, 0)
+        pltpu.make_async_copy(red_src.at[0], red_rep.at[rep], sum_recv.at[0]).start()
+
     def unit(step, carry):
         gain_sum, gate_sum = carry
         b = step // OWN_KV
@@ -323,8 +345,13 @@
             return total.astype(jnp.bfloat16)
 
         key_part = head_sum(d_logits, qblk).astype(jnp.float32)
+        gain_sum = gain_sum + jnp.sum(key_part * unit_key, axis=0, keepdims=True)
+
+        @pl.when(step == MICRO * OWN_KV - 1)
+        def _():
+            send_sums(gain_sum, gate_sum)
+
         value_part = head_sum(probs_low, dblk)
-        gain_sum = gain_sum + jnp.sum(key_part * unit_key, axis=0, keepdims=True)
         scaled = key_part * gain
         d_key = inverse * (scaled - unit_key * jnp.mean(scaled * unit_key, axis=-1, keepdims=True))
         gbuf[b, u, :, :, :HEAD] = d_key.astype(jnp.bfloat16).reshape(TILES, PATCH, HEAD)
@@ -338,37 +365,16 @@
         return gain_sum, gate_sum
 
     zero = jnp.zeros((1, HEAD), jnp.float32)
-    gain_sum, gate_sum = lax.fori_loop(0, MICRO * OWN_KV, unit, (zero, zero))
-
-    red_src[0, 0:1] = gain_sum
-    red_src[0, 1:2] = gate_sum
+    lax.fori_loop(0, MICRO * OWN_KV, unit, (zero, zero))
 
     def after_sums(i):
         for step in GRADS_AFTER[i]:
             send_grads(step // OWN_KV, step % OWN_KV)
 
-    def rep_copy(k):
-        return pltpu.make_async_remote_copy(
-            red_src.at[0], red_rep.at[rep], rep_send.at[k], sum_recv.at[0], device_id=rep_id(k)
-        )
-
-    def plane_copy(k):
-        return pltpu.make_async_remote_copy(
-            red_src.at[1], red_plane.at[me], plane_send.at[k], sum_recv.at[1], device_id={"mp": (me + k) % n_mp}
-        )
-
-    def rep_step(k, _):
-        @pl.when(k != rep)
-        def _():
-            rep_copy(k).start()
-        return 0
-
     def plane_step(k, _):
         plane_copy(k).start()
         return 0
 
-    lax.fori_loop(0, n_rep, rep_step, 0)
-    pltpu.make_async_copy(red_src.at[0], red_rep.at[rep], sum_recv.at[0]).start()
     for step in range(MICRO * OWN_KV - HOLD_A, MICRO * OWN_KV):
         send_attended(step // OWN_KV, step % OWN_KV)
     after_sums(0)

time: 72.2 us -> 71.3 us (0.988)
  Pallas kernels: 67.5 us -> 66.6 us
    pallas_call x1, Pallas kernels: 67.5 us -> 66.6 us  [shards(): pl.pallas_call(kernel, out_shape=(jax.ShapeDtypeStruct(queries.shape, bf1...]
where the time goes in v4:
time: 71.3 us; the launch traced here: 71.1 us
  Pallas kernels  66.6 us (93%)
  between operations  2.45 us (3%)
  local copies, waits for them, and re-layouts  2.1 us (3%)
    pallas_call x1, Pallas kernels, shards(): pl.pallas_call(kernel, out_shape=(jax.ShapeDtypeStruct(queries.shape, bf1...  66.6 us
    unnamed x3, local copies, waits for them, and re-layouts  2.1 us

profile of v4, /device:TPU:1, one launch (start us, length us, event | category | flops | bytes accessed | tf_op | source)
XLA Modules:
  0.0 71.1 jit_solution(18362091937905362474)
XLA Ops:
  1.3 66.6 %cross_attention.1 = (bf16[2,16,32,128]{3,2,1,0:T(8,128)(2,1)S(1)}, bf16[2,1,96,2048]{3,2,1,0:T(8,128)(2,1)S(1)}, f32[1,128]{1,0:T(1,128)S(1)}, f32[1,128]{1,0:T(1,128)S(1)}) custom-call(bf16[2,1,96,2048]{3,2,1,0:T(8,128)(2,1)} %kv_ref.1, f32[1,128]{1,0:T(1,128)} %bitcast.6, bf16[2,16,32,128]{3,2,1,0:T(8,128)(2,1)} %q_ref.1, s32[2,16,32]{2,1,0:T(8,128)} %count_ref.1, ...), custom_call_target="tpu_custom_call" | custom-call | tf_op jit(solution)/shard_map/cross_attention/pallas_call | solution.py:445
  67.9 0.7 copy.15
  68.6 0.9 %copy.16 = bf16[2,1,96,2048]{3,2,1,0:T(8,128)(2,1)} copy(bf16[2,1,96,2048]{3,2,1,0:T(8,128)(2,1)S(1)} %get-tuple-element.17) | data formatting | bytes 1572864
  69.4 0.5 copy.17

commit v5 on v4

--- a/solution.py
+++ b/solution.py
@@ -17,8 +17,8 @@
 OWN_HEADS = OWN_KV * GROUP
 ROWS = GROUP * TEXT
 WIDE = 2 * HEAD
-GRADS_AT_ONCE = 1
-GRADS_AFTER = ((1,), (2, 3))
+GRADS_AT_ONCE = (2, 1)
+GRADS_AFTER = (((), (2, 3)), ((1,), (2, 3)))
 ORDER = (
     (((0, 0), (0, 1)), ((1, 0),), ((1, 1),)),
     (((0, 0),), ((0, 1),), ((1, 0), (1, 1))),
@@ -358,7 +358,7 @@
         gbuf[b, u, :, :, HEAD:] = value_part.reshape(TILES, PATCH, HEAD)
 
 
-        @pl.when(step < GRADS_AT_ONCE)
+        @pl.when(step < jnp.where(first_half, GRADS_AT_ONCE[0], GRADS_AT_ONCE[1]))
         def _():
             send_grads(b, u)
 
@@ -368,8 +368,11 @@
     lax.fori_loop(0, MICRO * OWN_KV, unit, (zero, zero))
 
     def after_sums(i):
-        for step in GRADS_AFTER[i]:
-            send_grads(step // OWN_KV, step % OWN_KV)
+        for half, when in ((0, first_half), (1, jnp.logical_not(first_half))):
+            @pl.when(when)
+            def _():
+                for step in GRADS_AFTER[half][i]:
+                    send_grads(step // OWN_KV, step % OWN_KV)
 
     def plane_step(k, _):
         plane_copy(k).start()

time: 71.3 us -> 72.5 us (1.017); the launches traced: 71.1 us -> 71.3 us
  no operation moved by 1% of the time
where the time goes in v5:
time: 72.5 us; the launch traced here: 71.3 us
  Pallas kernels  66.7 us (92%)
  between operations  2.45 us (3%)
  local copies, waits for them, and re-layouts  2.1 us (3%)
    pallas_call x1, Pallas kernels, shards(): pl.pallas_call(kernel, out_shape=(jax.ShapeDtypeStruct(queries.shape, bf1...  66.7 us
    unnamed x3, local copies, waits for them, and re-layouts  2.1 us

profile of v5, /device:TPU:1, one launch (start us, length us, event | category | flops | bytes accessed | tf_op | source)
XLA Modules:
  0.0 71.3 jit_solution(17742140360538068195)
XLA Ops:
  1.3 66.7 %cross_attention.1 = (bf16[2,16,32,128]{3,2,1,0:T(8,128)(2,1)S(1)}, bf16[2,1,96,2048]{3,2,1,0:T(8,128)(2,1)S(1)}, f32[1,128]{1,0:T(1,128)S(1)}, f32[1,128]{1,0:T(1,128)S(1)}) custom-call(bf16[2,1,96,2048]{3,2,1,0:T(8,128)(2,1)} %kv_ref.1, f32[1,128]{1,0:T(1,128)} %bitcast.6, bf16[2,16,32,128]{3,2,1,0:T(8,128)(2,1)} %q_ref.1, s32[2,16,32]{2,1,0:T(8,128)} %count_ref.1, ...), custom_call_target="tpu_custom_call" | custom-call | tf_op jit(solution)/shard_map/cross_attention/pallas_call | solution.py:448
  68.0 0.7 copy.15
  68.7 0.9 %copy.16 = bf16[2,1,96,2048]{3,2,1,0:T(8,128)(2,1)} copy(bf16[2,1,96,2048]{3,2,1,0:T(8,128)(2,1)S(1)} %get-tuple-element.17) | data formatting | bytes 1572864
  69.6 0.5 copy.17
